TPU v7x, 32 devices: a whole 2x2x4 slice. The times are simulated.
32 devices in a mesh: dp: 4 (over y, core), seq: 8 (over z, x).
Axes of the slice: x: 2, y: 2, z: 4, core: 2. Of those that a mesh axis runs over, the one named last changes fastest.
Arguments:
- queries: bfloat16 [8, 512, 4096], P('dp', 'seq'), may hold values from -140 to 140
- keys: bfloat16 [8, 512, 4096], P('dp', 'seq'), may hold values from -5.5 to 5.5
- values: bfloat16 [8, 512, 4096], P('dp', 'seq'), may hold values from -6 to 6
- teacher: bfloat16 [8, 640, 1536], P('dp', 'seq'), may hold values from -6 to 6
- resample_index: int32 [8, 512, 4], P('dp', 'seq'), may hold values from 0 to 639, as said below
- resample_frac: int32 [8, 512, 2], P('dp', 'seq'), may hold values from 0 to 7
- timesteps: int32 [8], P('dp'), may hold values from 0 to 999
- norm_gain: float32 [4096], replicated, may hold values from 0.1 to 1.9
- proj_in: bfloat16 [4096, 1024], P(('dp', 'seq')), may hold values from -0.09375 to 0.09375
- bias_in: float32 [1024], replicated, may hold values from -3 to 3
- proj_out: bfloat16 [1024, 1536], P(('dp', 'seq')), may hold values from -0.1875 to 0.1875
- bias_out: float32 [1536], replicated, may hold values from -3 to 3
Outputs:
- alignment: float32 [8, 512], P('dp', 'seq')
- grad_attended: bfloat16 [8, 512, 4096], P('dp', 'seq')
Inputs may be any that keep to these rules, and one draw needn't show every extreme that they name: `resample_index`: every index of student token s lies in teacher rows (s // 64) * 80 - 8 to (s // 64 + 1) * 80 + 7.
All inputs are finite; a program needn't handle non-finite values.
Results may differ from a plain program's by a relative error of at most 0.0066.
Values may be sent and summed in bfloat16 or wider, within the bound.
A program may use at most 64 MiB of HBM per device.

v0:
```python
import math

import jax
import jax.numpy as jnp
from jax import lax
from jax.sharding import PartitionSpec as P

HD = 128
HALO = 8
TSTEPS = 1000


epsilon = 1e-06
loss_scale = 256.0


def padded_2(x, sides, width):
    for axis, dim in sides:
        size, length = (lax.axis_size(axis), x.shape[dim])
        up = [(i, (i + 1) % size) for i in range(size - 1)]
        down = [(j, i) for i, j in up]
        last = lax.slice_in_dim(x, length - width, length, axis=dim)
        leading = lax.slice_in_dim(x, 0, width, axis=dim)
        before = lax.ppermute(last, axis, up)
        after = lax.ppermute(leading, axis, down)
        x = jnp.concatenate([before, x, after], axis=dim)
    return x


def attend_items(triples):
    query_part, key_part, value_part = triples
    length = query_part.shape[1]
    local_width = query_part.shape[2]
    head_count = local_width // HD
    block_rows = min(length, 512)
    score_scale = HD ** (-0.5)

    def one_image(triple):
        query_img, key_img, value_img = triple
        key_heads = key_img.reshape(length, head_count, HD)
        value_heads = value_img.reshape(length, head_count, HD)
        query_blocks = query_img.reshape(length // block_rows, block_rows, head_count, HD)

        def one_block(query_block):
            scores = (
                jnp.einsum(
                    "qhd,khd->hqk", query_block, key_heads, preferred_element_type=jnp.float32
                )
                * score_scale
            )
            row_max = jnp.max(scores, axis=-1, keepdims=True)
            exp_scores = jnp.exp(scores - row_max)
            row_total = jnp.sum(exp_scores, axis=-1)
            prob_bf16 = exp_scores.astype(jnp.bfloat16)
            mixed_sum = jnp.einsum(
                "hqk,khd->qhd", prob_bf16, value_heads, preferred_element_type=jnp.float32
            )
            return (mixed_sum / jnp.transpose(row_total)[:, :, None]).astype(jnp.bfloat16)

        outputs = lax.map(one_block, query_blocks)
        return outputs.reshape(length, local_width)

    attended = lax.map(one_image, (query_part, key_part, value_part))
    return lax.all_to_all(attended, "seq", split_axis=1, concat_axis=2, tiled=True)


def shards(
    queries,
    keys,
    values,
    teacher,
    resample_index,
    resample_frac,
    timesteps,
    norm_gain,
    proj_in,
    bias_in,
    proj_out,
    bias_out,
):
    images_dev, rows_dev, model_width = queries.shape
    total_rows = images_dev * rows_dev
    attended = attend_items(
        (
            lax.all_to_all(queries, "seq", split_axis=2, concat_axis=1, tiled=True),
            lax.all_to_all(keys, "seq", split_axis=2, concat_axis=1, tiled=True),
            lax.all_to_all(values, "seq", split_axis=2, concat_axis=1, tiled=True),
        )
    )
    full_in, full_out = (
        lax.all_gather(proj_in, ("dp", "seq"), axis=0, tiled=True),
        lax.all_gather(proj_out, ("dp", "seq"), axis=0, tiled=True),
    )
    padded = padded_2(teacher, (("seq", 1),), HALO)
    att_wide = attended.reshape(total_rows, model_width).astype(jnp.float32)
    mean_square = jnp.mean(att_wide * att_wide, axis=-1, keepdims=True)
    inv_rms = lax.rsqrt(mean_square + epsilon)
    normed = (att_wide * inv_rms * norm_gain).astype(jnp.bfloat16)
    pre_act = jnp.dot(normed, full_in, preferred_element_type=jnp.float32) + bias_in
    hidden = jax.nn.silu(pre_act).astype(jnp.bfloat16)
    projected = jnp.dot(hidden, full_out, preferred_element_type=jnp.float32) + bias_out
    band_start = lax.axis_index("seq") * teacher.shape[1] - HALO
    local_index = (resample_index - band_start).reshape(images_dev, rows_dev * 4)
    picked = jnp.take_along_axis(padded, local_index[:, :, None], axis=1)
    picked = picked.reshape(total_rows, 4, padded.shape[2]).astype(jnp.float32)
    frac_x = resample_frac[:, :, 0].reshape(total_rows).astype(jnp.float32)
    frac_y = resample_frac[:, :, 1].reshape(total_rows).astype(jnp.float32)
    stencil = (
        jnp.stack(
            [
                (8.0 - frac_x) * (8.0 - frac_y),
                frac_x * (8.0 - frac_y),
                (8.0 - frac_x) * frac_y,
                frac_x * frac_y,
            ],
            axis=-1,
        )
        / 64.0
    )
    target = jnp.sum(stencil[:, :, None] * picked, axis=1)
    proj_norm = jnp.sqrt(jnp.sum(projected * projected, axis=-1, keepdims=True) + epsilon)
    target_norm = jnp.sqrt(jnp.sum(target * target, axis=-1, keepdims=True) + epsilon)
    alignment = jnp.sum(projected * target, axis=-1, keepdims=True) / (proj_norm * target_norm)
    image_weight = (
        0.25 + 0.75 * jnp.cos(0.5 * math.pi * timesteps.astype(jnp.float32) / TSTEPS) ** 2
    )
    time_weight = jnp.repeat(image_weight, rows_dev)[:, None]
    d_projected = (
        -loss_scale
        * time_weight
        * (target / (proj_norm * target_norm) - alignment * projected / (proj_norm * proj_norm))
    )
    d_proj_bf = d_projected.astype(jnp.bfloat16)
    d_hidden = lax.dot_general(
        d_proj_bf, full_out, (((1,), (1,)), ((), ())), preferred_element_type=jnp.float32
    )
    gate_sig = jax.nn.sigmoid(pre_act)
    d_pre = (d_hidden * gate_sig * (1.0 + pre_act * (1.0 - gate_sig))).astype(jnp.bfloat16)
    d_normed = lax.dot_general(
        d_pre, full_in, (((1,), (1,)), ((), ())), preferred_element_type=jnp.float32
    )
    gained = d_normed * norm_gain
    cubed = inv_rms * inv_rms * inv_rms
    grad_att = inv_rms * gained - att_wide * cubed * jnp.mean(
        att_wide * gained, axis=-1, keepdims=True
    )
    return (
        alignment.reshape(images_dev, rows_dev),
        grad_att.astype(jnp.bfloat16).reshape(images_dev, rows_dev, model_width),
    )


def solution(mesh):
    return jax.shard_map(
        shards,
        mesh=mesh,
        in_specs=(
            P("dp", "seq", None),
            P("dp", "seq", None),
            P("dp", "seq", None),
            P("dp", "seq", None),
            P("dp", "seq", None),
            P("dp", "seq", None),
            P("dp"),
            P(),
            P(("dp", "seq"), None),
            P(),
            P(("dp", "seq"), None),
            P(),
        ),
        out_specs=(P("dp", "seq"), P("dp", "seq", None)),
        check_vma=False,
    )
```

profile of v0, /device:TPU:0, one launch (start us, length us, event | category | flops | bytes accessed | tf_op | source)
XLA Modules:
  0.0 233.1 jit_solution(9449815165464318909)
XLA Ops:
  7.9 5.0 %copy.88 = bf16[2,64,4096]{1,0,2:T(2,128)(2,1)S(1)} copy(bf16[2,64,4096]{2,1,0:T(8,128)(2,1)} %param.14) | data formatting | bytes 2097152 | tf_op args[0]
  12.9 2.7 %reshape.286 = bf16[8,2,32768]{2,1,0:T(2,128)(2,1)} reshape(bf16[4096,2,64]{2,1,0:T(2,128)(2,1)S(1)} %bitcast.86) | data formatting | bytes 2097152
  15.6 7.3 %all-to-all-start.1 = ((bf16[8,2,32768]{2,1,0:T(2,128)(2,1)}), bf16[8,2,32768]{2,1,0:T(2,128)(2,1)S(1)}, u32[]{:S(2)}, u32[]{:S(2)}) async-start(bf16[8,2,32768]{2,1,0:T(2,128)(2,1)} %reshape.286), calls=%async_computation.1 | async-start | bytes 2097152 | tf_op jit(solution)/shard_map/all_to_all | solution.py:85
  22.9 5.1 %copy.91 = bf16[2,64,4096]{1,0,2:T(2,128)(2,1)S(1)} copy(bf16[2,64,4096]{2,1,0:T(8,128)(2,1)} %param.15) | data formatting | bytes 2097152 | tf_op args[1]
  27.9 2.7 %reshape.288 = bf16[8,2,32768]{2,1,0:T(2,128)(2,1)} reshape(bf16[4096,2,64]{2,1,0:T(2,128)(2,1)S(1)} %bitcast.87) | data formatting | bytes 2097152
  30.6 28.0 %all-to-all-done.1 = bf16[8,2,32768]{2,1,0:T(2,128)(2,1)S(1)} async-done(((bf16[8,2,32768]{2,1,0:T(2,128)(2,1)}), bf16[8,2,32768]{2,1,0:T(2,128)(2,1)S(1)}, u32[]{:S(2)}, u32[]{:S(2)}) %all-to-all-start.1) | async-done | bytes 1048608 | tf_op jit(solution)/shard_map/all_to_all | solution.py:85
  58.6 4.2 %all-to-all-start.2 = ((bf16[8,2,32768]{2,1,0:T(2,128)(2,1)}), bf16[8,2,32768]{2,1,0:T(2,128)(2,1)}, u32[]{:S(2)}, u32[]{:S(2)}) async-start(bf16[8,2,32768]{2,1,0:T(2,128)(2,1)} %reshape.288), calls=%async_computation.2 | async-start | bytes 2097152 | tf_op jit(solution)/shard_map/all_to_all | solution.py:86
  62.9 5.0 %copy.85 = bf16[2,64,4096]{1,0,2:T(2,128)(2,1)S(1)} copy(bf16[2,64,4096]{2,1,0:T(8,128)(2,1)} %param.16) | data formatting | bytes 2097152 | tf_op args[2]
  67.9 2.7 %reshape.284 = bf16[8,2,32768]{2,1,0:T(2,128)(2,1)} reshape(bf16[4096,2,64]{2,1,0:T(2,128)(2,1)S(1)} %bitcast.88) | data formatting | bytes 2097152
  70.6 33.1 %all-to-all-done.2 = bf16[8,2,32768]{2,1,0:T(2,128)(2,1)} async-done(((bf16[8,2,32768]{2,1,0:T(2,128)(2,1)}), bf16[8,2,32768]{2,1,0:T(2,128)(2,1)}, u32[]{:S(2)}, u32[]{:S(2)}) %all-to-all-start.2) | async-done | bytes 1048608 | tf_op jit(solution)/shard_map/all_to_all | solution.py:86
  103.7 4.3 %all-to-all-start = ((bf16[8,2,32768]{2,1,0:T(2,128)(2,1)}), bf16[8,2,32768]{2,1,0:T(2,128)(2,1)}, u32[]{:S(2)}, u32[]{:S(2)}) async-start(bf16[8,2,32768]{2,1,0:T(2,128)(2,1)} %reshape.284), calls=%async_computation | async-start | bytes 2097152 | tf_op jit(solution)/shard_map/all_to_all | solution.py:87
  108.9 3.7 %collective-permute-start = (bf16[2,8,1536]{2,1,0:T(8,128)(2,1)S(1)}, bf16[2,8,1536]{2,1,0:T(8,128)(2,1)S(1)}, u32[]{:S(2)}, u32[]{:S(2)}) collective-permute-start(bf16[2,8,1536]{2,1,0:T(8,128)(2,1)S(1)} %get-tuple-element.91), channel_id=1, source_target_pairs={{0,1},{1,2},{2,3},{3,4},{4,5},{5,6},{6,7},{8,9},{9,10},{10,11},{11... | collective-permute-start | bytes 147464 | tf_op jit(solution)/shard_map/ppermute | solution.py:24
  115.4 1.4 copy.110
  116.8 3.1 %reshape.289 = bf16[4096,2,64]{2,1,0:T(2,128)(2,1)S(1)} reshape(bf16[8,2,32768]{2,1,0:T(2,128)(2,1)} %all-to-all-done.2) | data formatting | bytes 2097152
  120.0 3.5 %copy.112 = bf16[2,64,8,512]{3,1,2,0:T(8,128)(2,1)} copy(bf16[2,64,8,512]{1,0,3,2:T(2,128)(2,1)S(1)} %bitcast.84) | data formatting | bytes 2097152 | tf_op jit(solution)/shard_map/all_to_all | solution.py:86
  123.5 11.5 %all-to-all-done = bf16[8,2,32768]{2,1,0:T(2,128)(2,1)} async-done(((bf16[8,2,32768]{2,1,0:T(2,128)(2,1)}), bf16[8,2,32768]{2,1,0:T(2,128)(2,1)}, u32[]{:S(2)}, u32[]{:S(2)}) %all-to-all-start) | async-done | bytes 1048608 | tf_op jit(solution)/shard_map/all_to_all | solution.py:87
  135.0 3.1 %reshape.285 = bf16[4096,2,64]{2,1,0:T(2,128)(2,1)S(1)} reshape(bf16[8,2,32768]{2,1,0:T(2,128)(2,1)} %all-to-all-done) | data formatting | bytes 2097152
  138.1 3.5 %copy.108 = bf16[2,64,8,512]{3,1,2,0:T(8,128)(2,1)} copy(bf16[2,64,8,512]{1,0,3,2:T(2,128)(2,1)S(1)} %bitcast.85) | data formatting | bytes 2097152 | tf_op jit(solution)/shard_map/all_to_all | solution.py:87
  141.6 17.7 %while.10 = (s32[]{:T(128)}, bf16[2,512,512]{1,2,0:T(8,128)(2,1)}, bf16[2,512,512]{2,1,0:T(8,128)(2,1)}, bf16[2,512,512]{2,1,0:T(8,128)(2,1)S(1)}, bf16[2,512,512]{2,1,0:T(8,128)(2,1)}, /*index=5*/s32[]{:T(128)}) while((s32[]{:T(128)}, bf16[2,512,512]{1,2,0:T(8,128)(2,1)}, bf16[2,512,512]{2,1,0:T(8,128)(2,1)}, ...), condition=%wide.region_3.0_spmd, body=%wide.region_0.3_spmd.sunk | while | flops 545779712 | bytes 51421376 | solution.py:63
  146.2 3.2 %fusion.60 = bf16[512,4,128]{0,2,1:T(8,128)(2,1)S(1)} fusion(bf16[512,4,128]{0,2,1:T(8,128)(2,1)S(1)} %bitcast.78, f32[4,512,512]{1,2,0:T(8,128)} %copy-done, f32[4,512]{1,0:T(4,128)S(1)} %get-tuple-element.139, f32[512,4]{0,1:T(4,128)S(1)} %bitcast.92), kind=kOutput, calls=%fused_computation.10.clone.1 | convolution fusion | flops 272105472 | bytes 5259264 | tf_op jit(solution)/shard_map/while/body/eval_jaxpr/while/body/eval_jaxpr/hqk,khd->qhd/dot_general | solution.py:55
  155.0 3.2 %fusion.60 = bf16[512,4,128]{0,2,1:T(8,128)(2,1)S(1)} fusion(bf16[512,4,128]{0,2,1:T(8,128)(2,1)S(1)} %bitcast.78, f32[4,512,512]{1,2,0:T(8,128)} %copy-done, f32[4,512]{1,0:T(4,128)S(1)} %get-tuple-element.139, f32[512,4]{0,1:T(4,128)S(1)} %bitcast.92), kind=kOutput, calls=%fused_computation.10.clone.1 | convolution fusion | flops 272105472 | bytes 5259264 | tf_op jit(solution)/shard_map/while/body/eval_jaxpr/while/body/eval_jaxpr/hqk,khd->qhd/dot_general | solution.py:55
  159.3 3.7 %copy.97 = bf16[2,512,512]{2,0,1:T(2,128)(2,1)} copy(bf16[2,512,512]{1,2,0:T(8,128)(2,1)} %get-tuple-element.44) | data formatting | bytes 2097152 | tf_op jit(solution)/shard_map/while | solution.py:63
  163.0 3.7 %all-to-all-start.3 = ((bf16[2,512,512]{2,0,1:T(2,128)(2,1)}), bf16[2,512,512]{2,0,1:T(2,128)(2,1)S(1)}, u32[]{:S(2)}, u32[]{:S(2)}) async-start(bf16[2,512,512]{2,0,1:T(2,128)(2,1)} %copy.97), calls=%async_computation.3 | async-start | bytes 2097152 | tf_op jit(solution)/shard_map/all_to_all | solution.py:64
  167.8 9.8 %gather_fusion = bf16[512,1536]{1,0:T(8,128)(2,1)} fusion(bf16[2,96,1536]{2,1,0:T(8,128)(2,1)S(1)} %pad_maximum_fusion, s32[512]{0:T(512)S(1)} %bitcast.74), kind=kCustom, calls=%fused_computation | custom fusion | bytes 3149824 | tf_op jit(solution)/shard_map/jit(take_along_axis)/gather | solution.py:104
  177.7 2.9 %gather.7 = bf16[128,4,1536]{2,1,0:T(4,128)(2,1)S(1)} reshape(bf16[512,1536]{1,0:T(8,128)(2,1)} %gather_fusion) | data formatting | bytes 3145728 | tf_op jit(solution)/shard_map/jit(take_along_axis)/gather | solution.py:104
  180.6 4.0 %multiply_reduce_fusion.1 = f32[128,1536]{1,0:T(8,128)} fusion(bf16[128,4,1536]{2,1,0:T(4,128)(2,1)S(1)} %gather.7, f32[128,4]{1,0:T(8,128)S(1)} %copy.100, pred[128,4]{1,0:T(8,128)(4,1)S(1)} %copy.102), kind=kLoop, calls=%fused_computation.17 | loop fusion | flops 2949120 | bytes 2361856 | tf_op jit(solution)/shard_map/reduce_sum | solution.py:120
  184.5 15.0 %all-to-all-done.3 = bf16[2,512,512]{2,0,1:T(2,128)(2,1)S(1)} async-done(((bf16[2,512,512]{2,0,1:T(2,128)(2,1)}), bf16[2,512,512]{2,0,1:T(2,128)(2,1)S(1)}, u32[]{:S(2)}, u32[]{:S(2)}) %all-to-all-start.3) | async-done | bytes 1048608 | tf_op jit(solution)/shard_map/all_to_all | solution.py:64
  201.1 1.6 copy.116
  203.3 5.6 %convolution_add_fusion.1 = f32[128,1024]{1,0:T(8,128)} fusion(bf16[4096,1024]{1,0:T(8,128)(2,1)} %all-gather.3.cloned.1.call-done, f32[128,4096]{1,0:T(8,128)S(1)} %bitcast.75, f32[4096]{0:T(1024)S(1)} %copy-done.8, f32[128]{0:T(128)S(1)} %rsqrt.15, f32[1024]{0:T(1024)S(1)} %copy-done.9), kind=kOutput, calls=%fused_computation.25 | convolution fusion | flops 1075445760 | bytes 11031040 | tf_op jit(solution)/shard_map/dot_general | solution.py:99
  208.8 3.6 %multiply_reduce_fusion.5 = (f32[128]{0:T(128)S(1)}, f32[128]{0:T(128)S(1)}, f32[128]{0:T(128)S(1)}, f32[128,1536]{1,0:T(8,128)}) fusion(f32[128,1536]{1,0:T(8,128)S(1)} %copy-done.6, f32[1536]{0:T(1024)S(1)} %copy-done.12, bf16[1024,1536]{1,0:T(8,128)(2,1)} %all-gather.5.cloned.1.call-done, f32[128,1024]{1,0:T(8,128)} %convolution_add_fusion.1), kind=kOutput, calls=%fused_computation.32 | convolution fusion | flops 404684416 | bytes 5250560 | tf_op jit(solution)/shard_map/dot_general | solution.py:101
  213.1 10.1 %multiply_reduce_fusion.2 = (f32[128]{0:T(128)S(1)}, f32[128,4096]{1,0:T(8,128)}) fusion(f32[128,4096]{1,0:T(8,128)S(1)} %bitcast.76, f32[4096]{0:T(1024)S(1)} %copy-done.8, bf16[4096,1024]{1,0:T(8,128)(2,1)} %all-gather.3.cloned.1.call-done, bf16[1024,1536]{1,0:T(8,128)(2,1)} %all-gather.5.cloned.1.call-done, f32[128,1024]{1,0:T(8,128)} %convolution_add_fusion.1, ...), kind=kOutput, calls=%fused_computation.20 | convolution fusion | flops 1480327040 | bytes 17844736 | tf_op jit(solution)/shard_map/dot_general | solution.py:139
  223.2 3.1 %subtract_convert_fusion = bf16[128,4096]{1,0:T(8,128)(2,1)} fusion(f32[128,4096]{1,0:T(8,128)S(1)} %bitcast.77, f32[128,4096]{1,0:T(8,128)} %get-tuple-element.100, f32[128]{0:T(128)S(1)} %broadcast_multiply_fusion, f32[128]{0:T(128)S(1)} %multiply_multiply_fusion, f32[128]{0:T(128)S(1)} %rsqrt.15), kind=kLoop, calls=%fused_computation.19 | loop fusion | flops 2621440 | bytes 5244416 | tf_op jit(solution)/shard_map/convert_element_type | solution.py:149
  (94 shorter events, 19.1 us)
Async XLA Ops:
  7.2 196.1 %all-gather.3.cloned.1.call-start = ((), (), s32[]{:S(2)}) async-start(), calls=%async_computation.4 | async-start | bytes 8650752 | tf_op jit(solution)/shard_map/all_gather | solution.py:91
  15.6 43.0 %all-to-all-start.1 = ((bf16[8,2,32768]{2,1,0:T(2,128)(2,1)}), bf16[8,2,32768]{2,1,0:T(2,128)(2,1)S(1)}, u32[]{:S(2)}, u32[]{:S(2)}) async-start(bf16[8,2,32768]{2,1,0:T(2,128)(2,1)} %reshape.286), calls=%async_computation.1 | async-start | bytes 2097152 | tf_op jit(solution)/shard_map/all_to_all | solution.py:85
  58.6 9.3 %copy-start.2 = (bf16[8,2,32768]{2,1,0:T(2,128)(2,1)}, bf16[8,2,32768]{2,1,0:T(2,128)(2,1)S(1)}, u32[]{:S(2)}) copy-start(bf16[8,2,32768]{2,1,0:T(2,128)(2,1)S(1)} %all-to-all-done.1) | copy-start | bytes 3145732
  58.6 45.1 %all-to-all-start.2 = ((bf16[8,2,32768]{2,1,0:T(2,128)(2,1)}), bf16[8,2,32768]{2,1,0:T(2,128)(2,1)}, u32[]{:S(2)}, u32[]{:S(2)}) async-start(bf16[8,2,32768]{2,1,0:T(2,128)(2,1)} %reshape.288), calls=%async_computation.2 | async-start | bytes 2097152 | tf_op jit(solution)/shard_map/all_to_all | solution.py:86
  70.6 43.3 %copy-start.3 = (bf16[8,2,32768]{2,1,0:T(2,128)(2,1)S(1)}, bf16[8,2,32768]{2,1,0:T(2,128)(2,1)}, u32[]{:S(2)}) copy-start(bf16[8,2,32768]{2,1,0:T(2,128)(2,1)} %copy-done.2) | copy-start | bytes 3145732
  103.7 31.2 %all-to-all-start = ((bf16[8,2,32768]{2,1,0:T(2,128)(2,1)}), bf16[8,2,32768]{2,1,0:T(2,128)(2,1)}, u32[]{:S(2)}, u32[]{:S(2)}) async-start(bf16[8,2,32768]{2,1,0:T(2,128)(2,1)} %reshape.284), calls=%async_computation | async-start | bytes 2097152 | tf_op jit(solution)/shard_map/all_to_all | solution.py:87
  108.0 100.9 %all-gather.5.cloned.1.call-start = ((), (), s32[]{:S(2)}) async-start(), calls=%async_computation.5 | async-start | bytes 3244032 | tf_op jit(solution)/shard_map/all_gather | solution.py:92
  108.9 58.9 %collective-permute-start = (bf16[2,8,1536]{2,1,0:T(8,128)(2,1)S(1)}, bf16[2,8,1536]{2,1,0:T(8,128)(2,1)S(1)}, u32[]{:S(2)}, u32[]{:S(2)}) collective-permute-start(bf16[2,8,1536]{2,1,0:T(8,128)(2,1)S(1)} %get-tuple-element.91), channel_id=1, source_target_pairs={{0,1},{1,2},{2,3},{3,4},{4,5},{5,6},{6,7},{8,9},{9,10},{10,11},{11... | collective-permute-start | bytes 147464 | tf_op jit(solution)/shard_map/ppermute | solution.py:24
  112.6 55.2 %collective-permute-start.1 = (bf16[2,8,1536]{2,1,0:T(8,128)(2,1)S(1)}, bf16[2,8,1536]{2,1,0:T(8,128)(2,1)S(1)}, u32[]{:S(2)}, u32[]{:S(2)}) collective-permute-start(bf16[2,8,1536]{2,1,0:T(8,128)(2,1)S(1)} %get-tuple-element.92), channel_id=1, source_target_pairs={{1,0},{2,1},{3,2},{4,3},{5,4},{6,5},{7,6},{9,8},{10,9},{11,10},{12... | collective-permute-start | bytes 147464 | tf_op jit(solution)/shard_map/ppermute | solution.py:25
  143.9 2.0 copy-start
  143.9 2.0 copy-start.1
  146.1 3.2 %copy-start.4 = (bf16[2,512,512]{1,2,0:T(8,128)(2,1)S(1)}, bf16[2,512,512]{1,2,0:T(8,128)(2,1)}, u32[]{:S(2)}) copy-start(bf16[2,512,512]{1,2,0:T(8,128)(2,1)} %get-tuple-element.147) | copy-start | bytes 3145732 | tf_op jit(solution)/shard_map/while
  149.4 1.0 copy-start.5
  152.7 2.0 copy-start
  152.7 2.0 copy-start.1
  155.0 3.2 %copy-start.4 = (bf16[2,512,512]{1,2,0:T(8,128)(2,1)S(1)}, bf16[2,512,512]{1,2,0:T(8,128)(2,1)}, u32[]{:S(2)}) copy-start(bf16[2,512,512]{1,2,0:T(8,128)(2,1)} %get-tuple-element.147) | copy-start | bytes 3145732 | tf_op jit(solution)/shard_map/while
  158.3 1.0 copy-start.5
  159.3 7.5 %copy-start.10 = (s32[2,64,4]{1,2,0:T(4,128)S(1)}, s32[2,64,4]{1,2,0:T(4,128)}, u32[]{:S(2)}) copy-start(s32[2,64,4]{1,2,0:T(4,128)} %param.18) | copy-start | bytes 6148
  159.3 7.6 %copy-start.11 = (s32[2,64,2]{1,2,0:T(2,128)S(1)}, s32[2,64,2]{1,2,0:T(2,128)}, u32[]{:S(2)}) copy-start(s32[2,64,2]{1,2,0:T(2,128)} %param.19) | copy-start | bytes 3076
  159.3 8.0 %copy-start.13 = (s32[2]{0:T(128)S(1)}, s32[2]{0:T(128)}, u32[]{:S(2)}) copy-start(s32[2]{0:T(128)} %param.20) | copy-start | bytes 28
  159.3 8.5 %copy-start.7 = (bf16[2,80,1536]{2,1,0:T(8,128)(2,1)S(1)}, bf16[2,80,1536]{2,1,0:T(8,128)(2,1)}, u32[]{:S(2)}) copy-start(bf16[2,80,1536]{2,1,0:T(8,128)(2,1)} %param.17) | copy-start | bytes 1474564
  163.0 36.6 %all-to-all-start.3 = ((bf16[2,512,512]{2,0,1:T(2,128)(2,1)}), bf16[2,512,512]{2,0,1:T(2,128)(2,1)S(1)}, u32[]{:S(2)}, u32[]{:S(2)}) async-start(bf16[2,512,512]{2,0,1:T(2,128)(2,1)} %copy.97), calls=%async_computation.3 | async-start | bytes 2097152 | tf_op jit(solution)/shard_map/all_to_all | solution.py:64
  201.1 2.2 copy-start.8
  201.1 2.1 copy-start.9
  203.2 5.6 %copy-start.6 = (f32[128,1536]{1,0:T(8,128)S(1)}, f32[128,1536]{1,0:T(8,128)}, u32[]{:S(2)}) copy-start(f32[128,1536]{1,0:T(8,128)} %multiply_reduce_fusion.1) | copy-start | bytes 2359300
  203.2 5.6 %copy-start.12 = (f32[1536]{0:T(1024)S(1)}, f32[1536]{0:T(1024)}, u32[]{:S(2)}) copy-start(f32[1536]{0:T(1024)} %param.25) | copy-start | bytes 18436
Sparse Core Ops, SparseCore 0:
  11.0 111.7 all-gather.2
  125.7 71.3 all-gather.4
where the time goes:
time: 234 us; the launch traced here: 233 us
  waiting for transfers between devices  88.3 us (38%)
  local copies, waits for them, and re-layouts  69.2 us (30%)
  matrix products  27.2 us (12%)
  starting transfers between devices  24.6 us (11%)
  between operations  14.3 us (6%)
  other arithmetic  9.26 us (4%)
    all_to_all x1, waiting for transfers between devices, shards(): lax.all_to_all(keys, 'seq', split_axis=2, concat_axis=1, tiled=True)  33.1 us
    unnamed x31, local copies, waits for them, and re-layouts  32.5 us
    all_to_all x1, waiting for transfers between devices, shards(): lax.all_to_all(queries, 'seq', split_axis=2, concat_axis=1, tiled=True)  28 us
    all_to_all x1, waiting for transfers between devices, attend_items(): lax.all_to_all(attended, 'seq', split_axis=1, concat_axis=2, tiled=True)  15 us
    gather x2, local copies, waits for them, and re-layouts, shards(): picked = jnp.take_along_axis(padded, local_index[:, :, None], axis=1)  12.7 us
    all_to_all x1, waiting for transfers between devices, shards(): lax.all_to_all(values, 'seq', split_axis=2, concat_axis=1, tiled=True)  11.5 us
    dot_general x1, matrix products, shards(): lax.dot_general(d_pre, full_in, (((1,), (1,)), ((), ())), preferred_eleme...  10.1 us
    all_to_all x1, starting transfers between devices, shards(): lax.all_to_all(queries, 'seq', split_axis=2, concat_axis=1, tiled=True)  7.25 us
  transfers between devices with their start and end apart: 8, of which 4 were waited for; matrix products, arithmetic and copies ran while one was open for 36% of the time, Pallas kernels for 0%

commit v1 on v0

v1 whole, which is shorter than its diff:
```python
import functools
import math

import jax
import jax.numpy as jnp
from jax import lax
from jax.experimental import pallas as pl
from jax.experimental.pallas import tpu as pltpu
from jax.sharding import PartitionSpec as P

HD = 128
HALO = 16
TSTEPS = 1000
MESH = pl.DeviceIdType.MESH

epsilon = 1e-06
loss_scale = 256.0
NT = (((1,), (1,)), ((), ()))


def attend_kernel(
    n, chunk, q_ref, k_ref, v_ref, t_ref, idx_ref, frac_ref, att_ref, target_ref,
    held, mixed, halo, send_sem, recv_sem, back_send, back_recv, halo_send, halo_recv,
):
    dp, me = lax.axis_index("dp"), lax.axis_index("seq")
    images, rows, width = q_ref.shape
    local = width // n
    chunks = local // chunk
    length = rows * n
    band = t_ref.shape[1]
    right, left = lax.rem(me + 1, n), lax.rem(me + n - 1, n)

    barrier = pltpu.get_barrier_semaphore()

    @pl.loop(1, n)
    def _(step):
        pl.semaphore_signal(
            barrier, inc=1, device_id=(dp, lax.rem(me + step, n)), device_id_type=MESH
        )

    pl.semaphore_wait(barrier, n - 1)

    sources = (q_ref, k_ref, v_ref)
    my_rows = pl.ds(pl.multiple_of(me * rows, rows), rows)

    def columns(owner, part):
        return pl.ds(pl.multiple_of(owner * local + part * chunk, chunk), chunk)

    halo_copies = [
        pltpu.make_async_remote_copy(
            src_ref=t_ref.at[:, pl.ds(start, HALO), :],
            dst_ref=halo.at[side],
            send_sem=halo_send.at[side],
            recv_sem=halo_recv.at[side],
            device_id=(dp, to),
            device_id_type=MESH,
        )
        for side, start, to in ((0, band - HALO, right), (1, 0, left))
    ]
    for copy in halo_copies:
        copy.start()
    for image in range(images):
        for part in range(chunks):
            for which, source in enumerate(sources):
                pltpu.make_async_copy(
                    source.at[image, :, columns(me, part)],
                    held.at[which, image, part, my_rows, :],
                    recv_sem.at[which, image, part],
                ).start()

                @pl.loop(1, n)
                def _(step, source=source, which=which, image=image, part=part):
                    to = lax.rem(me + step, n)
                    pltpu.make_async_remote_copy(
                        src_ref=source.at[image, :, columns(to, part)],
                        dst_ref=held.at[which, image, part, my_rows, :],
                        send_sem=send_sem.at[which],
                        recv_sem=recv_sem.at[which, image, part],
                        device_id=(dp, to),
                        device_id_type=MESH,
                    ).start()

    for copy in halo_copies:
        copy.wait()
    reach = band + 2 * HALO
    lane = lax.broadcasted_iota(jnp.int32, (rows, reach), 1) + (me * band - HALO)
    for image in range(images):
        index, frac = idx_ref[image], frac_ref[image].astype(jnp.float32)
        fx, fy = frac[:, 0:1], frac[:, 1:2]
        weights = ((8.0 - fx) * (8.0 - fy), fx * (8.0 - fy), (8.0 - fx) * fy, fx * fy)
        spread = jnp.zeros((rows, reach), jnp.float32)
        for j in range(4):
            spread += jnp.where(index[:, j : j + 1] == lane, weights[j], 0.0)
        spread = (spread * (1.0 / 64.0)).astype(jnp.bfloat16)
        before = jnp.where(me > 0, halo[0, image], jnp.zeros_like(halo[0, image]))
        after = jnp.where(me < n - 1, halo[1, image], jnp.zeros_like(halo[1, image]))
        near = jnp.concatenate([before, t_ref[image], after], axis=0)
        target_ref[pl.ds(image * rows, rows), :] = jnp.dot(
            spread, near, preferred_element_type=jnp.float32
        )

    block = min(length, 512)
    scale = HD ** (-0.5)
    for image in range(images):
        for part in range(chunks):
            for which in range(3):
                full = held.at[which, image, part]
                pltpu.make_async_copy(full, full, recv_sem.at[which, image, part]).wait()
            for head in range(chunk // HD):
                cols = pl.ds(head * HD, HD)
                key = held[1, image, part, :, cols]
                value = held[2, image, part, :, cols]
                for at in range(0, length, block):
                    query = held[0, image, part, pl.ds(at, block), cols]
                    scores = lax.dot_general(query, key, NT, preferred_element_type=jnp.float32)
                    top = jnp.max(scores, axis=-1, keepdims=True)
                    prob = jnp.exp((scores - top) * scale)
                    total = jnp.sum(prob, axis=-1, keepdims=True)
                    out = jnp.dot(
                        prob.astype(jnp.bfloat16), value, preferred_element_type=jnp.float32
                    )
                    mixed[image, part, pl.ds(at, block), cols] = (out / total).astype(jnp.bfloat16)
            pltpu.make_async_copy(
                mixed.at[image, part, my_rows, :],
                att_ref.at[image, :, columns(me, part)],
                back_recv,
            ).start()

            @pl.loop(1, n)
            def _(step, image=image, part=part):
                to = lax.rem(me + step, n)
                pltpu.make_async_remote_copy(
                    src_ref=mixed.at[image, part, pl.ds(pl.multiple_of(to * rows, rows), rows), :],
                    dst_ref=att_ref.at[image, :, columns(me, part)],
                    send_sem=back_send,
                    recv_sem=back_recv,
                    device_id=(dp, to),
                    device_id_type=MESH,
                ).start()

    for which, source in enumerate(sources):
        sent = source.at[:, :, pl.ds(0, width - local)]
        pltpu.make_async_copy(sent, sent, send_sem.at[which]).wait()
    sent = mixed.at[:, :, pl.ds(0, length - rows), :]
    pltpu.make_async_copy(sent, sent, back_send).wait()
    pltpu.make_async_copy(att_ref, att_ref, back_recv).wait()


def attend(n, queries, keys, values, teacher, index, frac):
    images, rows, width = queries.shape
    local = width // n
    chunk = min(local, 2 * HD)
    chunks = local // chunk
    length = rows * n
    vmem = pl.BlockSpec(memory_space=pltpu.VMEM)
    hbm = pl.BlockSpec(memory_space=pl.ANY)
    dma = pltpu.SemaphoreType.DMA
    return pl.pallas_call(
        functools.partial(attend_kernel, n, chunk),
        out_shape=(
            jax.ShapeDtypeStruct(queries.shape, jnp.bfloat16),
            jax.ShapeDtypeStruct((images * rows, teacher.shape[2]), jnp.float32),
        ),
        in_specs=[hbm, hbm, hbm, vmem, vmem, vmem],
        out_specs=(hbm, vmem),
        scratch_shapes=[
            pltpu.VMEM((3, images, chunks, length, chunk), jnp.bfloat16),
            pltpu.VMEM((images, chunks, length, chunk), jnp.bfloat16),
            pltpu.VMEM((2, images, HALO, teacher.shape[2]), jnp.bfloat16),
            dma((3,)),
            dma((3, images, chunks)),
            dma,
            dma,
            dma((2,)),
            dma((2,)),
        ],
        compiler_params=pltpu.CompilerParams(
            collective_id=0, has_side_effects=True, vmem_limit_bytes=40 * 2**20
        ),
        cost_estimate=pl.CostEstimate(
            flops=4 * images * length * length * local,
            bytes_accessed=300 * 2**20,
            transcendentals=images * length * length * local // HD,
        ),
        name="attend",
    )(queries, keys, values, teacher, index, frac)


def project_kernel(
    att_ref, target_ref, tw_ref, gain_ref, bias_in_ref, bias_out_ref, in_hbm, out_hbm,
    align_ref, grad_ref, in_ref, out_ref, in_sem, out_sem,
):
    images, rows, width = att_ref.shape
    total = images * rows
    depth = in_hbm.shape[0] // in_sem.shape[0]
    count = in_sem.shape[0]

    in_copies = [
        pltpu.make_async_copy(
            in_hbm.at[pl.ds(c * depth, depth), :], in_ref.at[pl.ds(c * depth, depth), :], in_sem.at[c]
        )
        for c in range(count)
    ]
    out_copy = pltpu.make_async_copy(out_hbm, out_ref, out_sem)
    for copy in in_copies:
        copy.start()
    out_copy.start()

    def attended(c):
        return att_ref[:, :, pl.ds(c * depth, depth)].reshape(total, depth).astype(jnp.float32)

    squares = jnp.zeros((total, 1), jnp.float32)
    for c in range(count):
        wide = attended(c)
        squares += jnp.sum(wide * wide, axis=-1, keepdims=True)
    inv_rms = lax.rsqrt(squares / width + epsilon)

    raw = jnp.zeros((total, in_hbm.shape[1]), jnp.float32)
    for c in range(count):
        normed = (attended(c) * inv_rms * gain_ref[:, pl.ds(c * depth, depth)]).astype(jnp.bfloat16)
        in_copies[c].wait()
        raw += jnp.dot(
            normed, in_ref[pl.ds(c * depth, depth), :], preferred_element_type=jnp.float32
        )
    pre_act = raw + bias_in_ref[...]
    gate = 1.0 / (1.0 + jnp.exp(-pre_act))
    hidden = (pre_act * gate).astype(jnp.bfloat16)
    out_copy.wait()
    projected = (
        jnp.dot(hidden, out_ref[...], preferred_element_type=jnp.float32) + bias_out_ref[...]
    )
    target = target_ref[...]
    pp = jnp.sum(projected * projected, axis=-1, keepdims=True) + epsilon
    tt = jnp.sum(target * target, axis=-1, keepdims=True) + epsilon
    pt = jnp.sum(projected * target, axis=-1, keepdims=True)
    both = lax.rsqrt(pp) * lax.rsqrt(tt)
    alignment = pt * both
    spread = jnp.transpose(jnp.broadcast_to(alignment, (total, 128)))
    for image in range(images):
        align_ref[image : image + 1, :] = spread[0:1, image * rows : (image + 1) * rows]
    factor = -loss_scale * tw_ref[...]
    d_proj = (factor * both * target - (factor * alignment / pp) * projected).astype(jnp.bfloat16)
    d_hidden = lax.dot_general(d_proj, out_ref[...], NT, preferred_element_type=jnp.float32)
    d_pre = (d_hidden * gate * (1.0 + pre_act * (1.0 - gate))).astype(jnp.bfloat16)
    mean = jnp.sum(d_pre.astype(jnp.float32) * raw, axis=-1, keepdims=True) / (inv_rms * width)
    pull = inv_rms * inv_rms * inv_rms * mean
    for c in range(count):
        cols = pl.ds(c * depth, depth)
        d_normed = lax.dot_general(
            d_pre, in_ref[cols, :], NT, preferred_element_type=jnp.float32
        )
        grad = inv_rms * gain_ref[:, cols] * d_normed - attended(c) * pull
        grad_ref[:, :, cols] = grad.astype(jnp.bfloat16).reshape(images, rows, depth)


def project(att, target, time_weight, gain, bias_in, bias_out, full_in, full_out):
    images, rows, width = att.shape
    vmem = pl.BlockSpec(memory_space=pltpu.VMEM)
    hbm = pl.BlockSpec(memory_space=pl.ANY)
    dma = pltpu.SemaphoreType.DMA
    return pl.pallas_call(
        project_kernel,
        out_shape=(
            jax.ShapeDtypeStruct((images, rows), jnp.float32),
            jax.ShapeDtypeStruct(att.shape, jnp.bfloat16),
        ),
        in_specs=[vmem] * 6 + [hbm, hbm],
        out_specs=(vmem, vmem),
        scratch_shapes=[
            pltpu.VMEM(full_in.shape, jnp.bfloat16),
            pltpu.VMEM(full_out.shape, jnp.bfloat16),
            dma((8,)),
            dma,
        ],
        compiler_params=pltpu.CompilerParams(vmem_limit_bytes=40 * 2**20),
        name="project",
    )(att, target, time_weight, gain, bias_in, bias_out, full_in, full_out)


def shards(
    queries,
    keys,
    values,
    teacher,
    resample_index,
    resample_frac,
    timesteps,
    norm_gain,
    proj_in,
    bias_in,
    proj_out,
    bias_out,
):
    rows = queries.shape[1]
    full_in = lax.all_gather(proj_in, ("dp", "seq"), axis=0, tiled=True)
    full_out = lax.all_gather(proj_out, ("dp", "seq"), axis=0, tiled=True)
    image_weight = (
        0.25 + 0.75 * jnp.cos(0.5 * math.pi * timesteps.astype(jnp.float32) / TSTEPS) ** 2
    )
    time_weight = jnp.repeat(image_weight, rows)[:, None]
    att, target = attend(
        lax.axis_size("seq"), queries, keys, values, teacher, resample_index, resample_frac
    )
    return project(
        att, target, time_weight, norm_gain[None], bias_in[None], bias_out[None], full_in, full_out
    )


def solution(mesh):
    return jax.shard_map(
        shards,
        mesh=mesh,
        in_specs=(
            P("dp", "seq", None),
            P("dp", "seq", None),
            P("dp", "seq", None),
            P("dp", "seq", None),
            P("dp", "seq", None),
            P("dp", "seq", None),
            P("dp"),
            P(),
            P(("dp", "seq"), None),
            P(),
            P(("dp", "seq"), None),
            P(),
        ),
        out_specs=(P("dp", "seq"), P("dp", "seq", None)),
        check_vma=False,
    )
```

time: 234 us -> 201 us (0.86)
  Pallas kernels: 0 us -> 139 us
  local copies, waits for them, and re-layouts: 69.2 us -> 13.9 us
  waiting for transfers between devices: 88.3 us -> 33.4 us
  matrix products: 27.2 us -> 0 us
  starting transfers between devices: 24.6 us -> 0.08 us
  other arithmetic: 9.26 us -> 0.7 us
    pallas_call x0 -> x2, Pallas kernels: none -> 139 us  [the longest x1 130 us: attend(): pl.pallas_call(functools.partial(attend_kernel, n, chunk), out_shape=(jax...]
    all_to_all x4 -> x0, waiting for transfers between devices: 87.6 us -> none  [the longest x1 33.1 us: shards(): lax.all_to_all(keys, 'seq', split_axis=2, concat_axis=1, tiled=True)]
    all_gather x2, waiting for transfers between devices: 0.01 us -> 32 us  [the longest x1 32 us: shards(): full_in = lax.all_gather(proj_in, ('dp', 'seq'), axis=0, tiled=True)]
    dot_general x7 -> x0, matrix products: 27.2 us -> none  [the longest x1 10.1 us: shards(): lax.dot_general(d_pre, full_in, (((1,), (1,)), ((), ())), preferred_eleme...]
    unnamed x31 -> x18, local copies, waits for them, and re-layouts: 32.5 us -> 12.9 us
    all_to_all x4 -> x0, starting transfers between devices: 19.5 us -> none  [the longest x1 7.25 us: shards(): lax.all_to_all(queries, 'seq', split_axis=2, concat_axis=1, tiled=True)]
    gather x2 -> x0, local copies, waits for them, and re-layouts: 12.7 us -> none  [shards(): picked = jnp.take_along_axis(padded, local_index[:, :, None], axis=1)]
    all_to_all x3 -> x0, local copies, waits for them, and re-layouts: 8.47 us -> none  [the longest x1 3.52 us: shards(): lax.all_to_all(values, 'seq', split_axis=2, concat_axis=1, tiled=True)]
  transfers between devices with their start and end apart: 8 -> 2, of which waited for: 4 -> 1; matrix products, arithmetic and copies ran while one was open for 36% -> 2% of each run, Pallas kernels for 0% -> 65%
where the time goes in v1:
time: 201 us
  Pallas kernels  139 us (69%)
  waiting for transfers between devices  33.4 us (17%)
  between operations  14.1 us (7%)
  local copies, waits for them, and re-layouts  13.9 us (7%)
    pallas_call x1, Pallas kernels, attend(): pl.pallas_call(functools.partial(attend_kernel, n, chunk), out_shape=(jax...  130 us
    all_gather x1, waiting for transfers between devices, shards(): full_in = lax.all_gather(proj_in, ('dp', 'seq'), axis=0, tiled=True)  32 us
    unnamed x18, local copies, waits for them, and re-layouts  12.9 us
    pallas_call x1, Pallas kernels, project(): pl.pallas_call(project_kernel, out_shape=(jax.ShapeDtypeStruct((images, r...  8.88 us
  transfers between devices with their start and end apart: 2, of which 1 were waited for; matrix products, arithmetic and copies ran while one was open for 2% of the time, Pallas kernels for 65%

profile of v1, /device:TPU:0, one launch (start us, length us, event | category | flops | bytes accessed | tf_op | source)
XLA Modules:
  0.0 200.7 jit_solution(8689018148509462623)
XLA Ops:
  7.2 0.0 all-gather.5.cloned.1.call-start
  7.2 0.7 all-gather.5.cloned.1.call-update
  7.9 0.0 all-gather.3.cloned.1.call-start
  7.9 0.7 all-gather.3.cloned.1.call-update
  8.6 0.7 broadcast_in_dim.15.bias_out_ref
  9.3 0.7 multiply_add_fusion
  10.0 0.1 broadcast_in_dim.12
  10.1 0.1 broadcast_in_dim_reshape.4.tw_ref
  10.3 0.8 copy.14.idx_ref
  11.1 0.8 copy.15.frac_ref
  11.8 0.0 copy-start.4
  11.9 1.2 copy-done.4
  13.1 0.0 copy-start.5
  13.1 1.2 copy-done.5
  14.3 0.0 copy-start.6
  14.3 1.2 copy-done.6
  15.5 0.0 copy-start.7
  15.5 1.0 copy-done.7
  16.6 129.7 %attend.1 = (bf16[2,64,4096]{2,1,0:T(8,128)(2,1)S(1)}, f32[128,1536]{1,0:T(8,128)S(1)}) custom-call(bf16[2,64,4096]{2,1,0:T(8,128)(2,1)S(1)} %copy-done.4, bf16[2,64,4096]{2,1,0:T(8,128)(2,1)S(1)} %copy-done.5, bf16[2,64,4096]{2,1,0:T(8,128)(2,1)S(1)} %copy-done.6, bf16[2,80,1536]{2,1,0:T(8,128)(2,1)S(1)} %copy-done.7, s32[2,64,4]{2,1,0:T(8,128)S(1)} %copy.14.idx_ref, ...), custom_call_target="tpu_custom_call" | custom-call | flops 1073741824 | bytes 314572800 | tf_op jit(solution)/shard_map/attend/pallas_call | solution.py:158
  146.3 0.0 all-gather.5.cloned.1.call-done.out_hbm
  146.3 32.0 %all-gather.3.cloned.1.call-done.in_hbm = bf16[4096,1024]{1,0:T(8,128)(2,1)} async-done(((bf16[128,1024]{1,0:T(8,128)(2,1)}), bf16[4096,1024]{1,0:T(8,128)(2,1)}) %all-gather.3.cloned.1.call-update) | async-done | bytes 8388624 | tf_op jit(solution)/shard_map/all_gather | solution.py:295
  178.3 0.0 copy-start
  178.3 3.4 %copy-done = bf16[4096,1024]{1,0:T(8,128)(2,1)S(1)} copy-done((bf16[4096,1024]{1,0:T(8,128)(2,1)S(1)}, bf16[4096,1024]{1,0:T(8,128)(2,1)}, u32[]{:S(2)}) %copy-start) | copy-done | bytes 8388632
  181.7 0.0 copy-start.1
  181.7 1.9 copy-done.1
  183.6 0.0 copy-start.2
  183.6 0.7 copy-done.2
  184.3 0.0 copy-start.3
  184.3 0.7 copy-done.3
  185.0 8.9 %project.1 = (f32[2,64]{1,0:T(2,128)}, bf16[2,64,4096]{2,1,0:T(8,128)(2,1)}) custom-call(bf16[2,64,4096]{2,1,0:T(8,128)(2,1)S(1)} %get-tuple-element.4.att_ref, f32[128,1536]{1,0:T(8,128)S(1)} %get-tuple-element.5.target_ref, f32[128,1]{1,0:T(8,128)S(1)} %broadcast_in_dim_reshape.4.tw_ref, f32[1,4096]{1,0:T(1,128)S(1)} %bitcast.2, f32[1,1024]{1,0:T(1,128)S(1)} %bitcast.3, ...), custom_call_target="tpu_custom_call" | custom-call | tf_op jit(solution)/shard_map/project/pallas_call | solution.py:261
Async XLA Ops:
  7.2 139.1 %all-gather.5.cloned.1.call-start = ((), (), s32[]{:S(2)}) async-start(), calls=%async_computation.1 | async-start | bytes 3244032 | tf_op jit(solution)/shard_map/all_gather | solution.py:296
  7.9 170.4 %all-gather.3.cloned.1.call-start = ((), (), s32[]{:S(2)}) async-start(), calls=%async_computation | async-start | bytes 8650752 | tf_op jit(solution)/shard_map/all_gather | solution.py:295
  11.8 1.2 copy-start.4
  13.1 1.2 copy-start.5
  14.3 1.2 copy-start.6
  15.5 1.0 copy-start.7
  178.3 3.4 %copy-start = (bf16[4096,1024]{1,0:T(8,128)(2,1)S(1)}, bf16[4096,1024]{1,0:T(8,128)(2,1)}, u32[]{:S(2)}) copy-start(bf16[4096,1024]{1,0:T(8,128)(2,1)} %all-gather.3.cloned.1.call-done.in_hbm) | copy-start | bytes 25165828
  181.7 1.9 copy-start.1
  183.6 0.7 copy-start.2
  184.3 0.7 copy-start.3
Sparse Core Ops, SparseCore 0:
  11.0 78.2 all-gather.4
  92.3 85.9 all-gather.2

commit v2 on v1

v2 whole, which is shorter than its diff:
```python
import functools
import math

import jax
import jax.numpy as jnp
from jax import lax
from jax.experimental import pallas as pl
from jax.experimental.pallas import tpu as pltpu
from jax.sharding import PartitionSpec as P

HD = 128
HALO = 16
TSTEPS = 1000
MESH = pl.DeviceIdType.MESH

epsilon = 1e-06
loss_scale = 256.0
NT = (((1,), (1,)), ((), ()))


def align_kernel(
    n, chunk, gather,
    q_ref, k_ref, v_ref, t_ref, idx_ref, frac_ref, step_ref, gain_hbm, bias_in_hbm, bias_out_hbm,
    in_hbm, out_hbm,
    align_ref, grad_ref,
    held, mixed, att_ref, target_ref, near, in_ref, out_ref, gain_ref, bias_in_ref, bias_out_ref,
    send_sem, recv_sem, back_send, back_recv, halo_send, halo_recv, near_sem, small_sem,
    w_local, w_recv, line_send, side_send,
):
    dp, me = lax.axis_index("dp"), lax.axis_index("seq")
    images, rows, width = q_ref.shape
    total = images * rows
    local = width // n
    chunks = local // chunk
    length = rows * n
    band = t_ref.shape[1]
    reach = band + 2 * HALO
    right, left = lax.rem(me + 1, n), lax.rem(me + n - 1, n)
    here = dp * n + me
    weights = ((in_ref, in_hbm.shape[0]), (out_ref, out_hbm.shape[0]))

    def piece(j, block, count=1):
        ref, size = weights[j]
        return ref.at[pl.ds(pl.multiple_of(block * size, size), count * size), :]

    own = here if gather else 0
    w_copies = [
        pltpu.make_async_copy(source, piece(j, own), w_local.at[j])
        for j, source in enumerate((in_hbm, out_hbm))
    ]
    near_copy = pltpu.make_async_copy(t_ref, near.at[:, pl.ds(HALO, band), :], near_sem)
    small_copies = [
        pltpu.make_async_copy(source, dest, small_sem.at[j])
        for j, (source, dest) in enumerate(
            ((gain_hbm, gain_ref), (bias_in_hbm, bias_in_ref), (bias_out_hbm, bias_out_ref))
        )
    ]
    for copy in w_copies + [near_copy] + small_copies:
        copy.start()

    barrier = pltpu.get_barrier_semaphore()

    @pl.loop(1, n)
    def _(step):
        pl.semaphore_signal(
            barrier, inc=1, device_id=(dp, lax.rem(me + step, n)), device_id_type=MESH
        )

    greeted = n - 1
    if gather:
        core, y = lax.rem(dp, 2), lax.div(dp, 2)
        x, z = lax.rem(me, 2), lax.div(me, 2)
        lines = n // 2
        sibling = (y * 2 + (1 - core), me)
        across_y = ((1 - y) * 2 + core, me)
        across_x = (dp, z * 2 + (1 - x))
        for partner in (sibling, across_y):
            pl.semaphore_signal(barrier, inc=1, device_id=partner, device_id_type=MESH)
        greeted += 2
    pl.semaphore_wait(barrier, greeted)

    def push(block, device, sems):
        for j in range(2):
            pltpu.make_async_remote_copy(
                src_ref=piece(j, block),
                dst_ref=piece(j, block),
                send_sem=sems[j],
                recv_sem=w_recv.at[j, block],
                device_id=device,
                device_id_type=MESH,
            ).start()

    def arrived(block):
        for j in range(2):
            pltpu.make_async_copy(piece(j, block), piece(j, block), w_recv.at[j, block]).wait()

    def line_sems(side, step):
        return [line_send.at[side, step, j] for j in range(2)]

    def side_sems(kind):
        return [side_send.at[kind, j] for j in range(2)]

    def block_at(y_of, core_of, z_of, x_of):
        return (y_of * 2 + core_of) * n + z_of * 2 + x_of

    def spread_from_line(block):
        push(block, across_y, side_sems(1))
        push(block, across_x, side_sems(0))
        push(block, sibling, side_sems(2))

    def at_distance(step, act):
        if step == 0:
            act(z, 0)
            return

        @pl.when(z - step >= 0)
        def _():
            act(z - step, 1)

        @pl.when(z + step < lines)
        def _():
            act(z + step, 2)

    def go_on(step, z_of, come_from):
        block = block_at(y, core, z_of, x)
        if come_from != 0:
            arrived(block)
        if come_from != 2:
            @pl.when(z + 1 < lines)
            def _():
                push(block, (dp, me + 2), line_sems(0, step))
        if come_from != 1:
            @pl.when(z >= 1)
            def _():
                push(block, (dp, me - 2), line_sems(1, step))
        spread_from_line(block)

    def line_stage(step):
        at_distance(step, lambda z_of, side: go_on(step, z_of, side))

    def x_stage(step):
        def act(z_of, side):
            block = block_at(y, core, z_of, 1 - x)
            arrived(block)
            push(block, across_y, side_sems(1))
            push(block, sibling, side_sems(2))

        at_distance(step, act)

    def y_stage(step):
        def act(z_of, side):
            for x_of in (x, 1 - x):
                block = block_at(1 - y, core, z_of, x_of)
                arrived(block)
                push(block, sibling, side_sems(2))

        at_distance(step, act)

    def weight_stage(slot):
        if not gather:
            return
        if slot < lines:
            line_stage(slot)
        if 1 <= slot <= lines:
            x_stage(slot - 1)
        if 3 <= slot <= lines + 2:
            y_stage(slot - 3)

    sources = (q_ref, k_ref, v_ref)
    my_rows = pl.ds(pl.multiple_of(me * rows, rows), rows)

    def columns(owner, part):
        return pl.ds(pl.multiple_of(owner * local + part * chunk, chunk), chunk)

    work = [(image, part) for image in range(images) for part in range(chunks)]

    def issue(at):
        if at >= len(work):
            return
        image, part = work[at]
        for which, source in enumerate(sources):
            pltpu.make_async_copy(
                source.at[image, :, columns(me, part)],
                held.at[which, image, part, my_rows, :],
                recv_sem.at[which, image, part],
            ).start()

        @pl.loop(1, n)
        def _(step):
            to = lax.rem(me + step, n)
            for which, source in enumerate(sources):
                pltpu.make_async_remote_copy(
                    src_ref=source.at[image, :, columns(to, part)],
                    dst_ref=held.at[which, image, part, my_rows, :],
                    send_sem=send_sem.at[which],
                    recv_sem=recv_sem.at[which, image, part],
                    device_id=(dp, to),
                    device_id_type=MESH,
                ).start()

    halo_copies = [
        pltpu.make_async_remote_copy(
            src_ref=t_ref.at[:, pl.ds(start, HALO), :],
            dst_ref=near.at[:, pl.ds(land, HALO), :],
            send_sem=halo_send.at[side],
            recv_sem=halo_recv.at[side],
            device_id=(dp, to),
            device_id_type=MESH,
        )
        for side, start, land, to in ((0, band - HALO, 0, right), (1, 0, band + HALO, left))
    ]
    for copy in w_copies:
        if gather:
            copy.wait()
    for copy in halo_copies:
        copy.start()
    weight_stage(0)
    issue(0)

    near_copy.wait()
    for copy in halo_copies:
        copy.wait()
    row = lax.broadcasted_iota(jnp.int32, (reach, rows), 0) + (me * band - HALO)
    real = lax.broadcasted_iota(jnp.int32, (reach, near.shape[2]), 0) + (me * band - HALO)
    real = jnp.logical_and(real >= 0, real < n * band)
    for image in range(images):
        index, frac = idx_ref[image], frac_ref[image].astype(jnp.float32)
        fx, fy = frac[0:1, :], frac[1:2, :]
        factors = ((8.0 - fx) * (8.0 - fy), fx * (8.0 - fy), (8.0 - fx) * fy, fx * fy)
        spread = jnp.zeros((reach, rows), jnp.float32)
        for j in range(4):
            spread += jnp.where(index[j : j + 1, :] == row, factors[j], 0.0)
        spread = (spread * (1.0 / 64.0)).astype(jnp.bfloat16)
        wide = jnp.where(real, near[image].astype(jnp.float32), 0.0).astype(jnp.bfloat16)
        target_ref[pl.ds(image * rows, rows), :] = lax.dot_general(
            spread, wide, (((0,), (0,)), ((), ())), preferred_element_type=jnp.float32
        )
    weight_stage(1)
    issue(1)

    block_rows = min(length, 512)
    scale = HD ** (-0.5)
    for at, (image, part) in enumerate(work):
        for which in range(3):
            full = held.at[which, image, part]
            pltpu.make_async_copy(full, full, recv_sem.at[which, image, part]).wait()
        issue(at + 2)
        for head in range(chunk // HD):
            cols = pl.ds(head * HD, HD)
            key = held[1, image, part, :, cols]
            value = held[2, image, part, :, cols]
            for start in range(0, length, block_rows):
                query = held[0, image, part, pl.ds(start, block_rows), cols]
                scores = lax.dot_general(query, key, NT, preferred_element_type=jnp.float32)
                top = jnp.max(scores, axis=-1, keepdims=True)
                prob = jnp.exp((scores - top) * scale)
                mass = jnp.sum(prob, axis=-1, keepdims=True)
                out = jnp.dot(prob.astype(jnp.bfloat16), value, preferred_element_type=jnp.float32)
                mixed[image, part, pl.ds(start, block_rows), cols] = (out / mass).astype(
                    jnp.bfloat16
                )
        pltpu.make_async_copy(
            mixed.at[image, part, my_rows, :], att_ref.at[image, :, columns(me, part)], back_recv
        ).start()

        @pl.loop(1, n)
        def _(step, image=image, part=part):
            to = lax.rem(me + step, n)
            pltpu.make_async_remote_copy(
                src_ref=mixed.at[image, part, pl.ds(pl.multiple_of(to * rows, rows), rows), :],
                dst_ref=att_ref.at[image, :, columns(me, part)],
                send_sem=back_send,
                recv_sem=back_recv,
                device_id=(dp, to),
                device_id_type=MESH,
            ).start()

        weight_stage(at + 2)

    if gather:
        for slot in range(len(work) + 2, lines + 3):
            weight_stage(slot)
    pltpu.make_async_copy(att_ref, att_ref, back_recv).wait()

    for copy in small_copies:
        copy.wait()
    if gather:
        @pl.loop(0, n)
        def _(at):
            for y_of in range(2):
                arrived((y_of * 2 + (1 - core)) * n + at)
    else:
        for copy in w_copies:
            copy.wait()

    depth = in_ref.shape[0] // 8

    def attended(c):
        return att_ref[:, :, pl.ds(c * depth, depth)].reshape(total, depth).astype(jnp.float32)

    squares = jnp.zeros((total, 1), jnp.float32)
    for c in range(8):
        wide = attended(c)
        squares += jnp.sum(wide * wide, axis=-1, keepdims=True)
    inv_rms = lax.rsqrt(squares / width + epsilon)

    raw = jnp.zeros((total, in_ref.shape[1]), jnp.float32)
    for c in range(8):
        normed = (attended(c) * inv_rms * gain_ref[:, pl.ds(c * depth, depth)]).astype(jnp.bfloat16)
        raw += jnp.dot(
            normed, in_ref[pl.ds(c * depth, depth), :], preferred_element_type=jnp.float32
        )
    pre_act = raw + bias_in_ref[...]
    gate = 1.0 / (1.0 + jnp.exp(-pre_act))
    hidden = (pre_act * gate).astype(jnp.bfloat16)
    projected = (
        jnp.dot(hidden, out_ref[...], preferred_element_type=jnp.float32) + bias_out_ref[...]
    )
    target = target_ref[...]
    pp = jnp.sum(projected * projected, axis=-1, keepdims=True) + epsilon
    tt = jnp.sum(target * target, axis=-1, keepdims=True) + epsilon
    pt = jnp.sum(projected * target, axis=-1, keepdims=True)
    both = lax.rsqrt(pp) * lax.rsqrt(tt)
    alignment = pt * both
    turned = jnp.transpose(jnp.broadcast_to(alignment, (total, 128)))
    for image in range(images):
        align_ref[image : image + 1, :] = turned[0:1, image * rows : (image + 1) * rows]
    steps = jnp.concatenate(
        [jnp.full((rows, 1), step_ref[image], jnp.int32) for image in range(images)], axis=0
    )
    wave = jnp.cos(0.5 * math.pi * steps.astype(jnp.float32) / TSTEPS)
    factor = -loss_scale * (0.25 + 0.75 * wave * wave)
    d_proj = (factor * both * target - (factor * alignment / pp) * projected).astype(jnp.bfloat16)
    d_hidden = lax.dot_general(d_proj, out_ref[...], NT, preferred_element_type=jnp.float32)
    d_pre = (d_hidden * gate * (1.0 + pre_act * (1.0 - gate))).astype(jnp.bfloat16)
    mean = jnp.sum(d_pre.astype(jnp.float32) * raw, axis=-1, keepdims=True) / (inv_rms * width)
    pull = inv_rms * inv_rms * inv_rms * mean
    for c in range(8):
        cols = pl.ds(c * depth, depth)
        d_normed = lax.dot_general(d_pre, in_ref[cols, :], NT, preferred_element_type=jnp.float32)
        grad = inv_rms * gain_ref[:, cols] * d_normed - attended(c) * pull
        grad_ref[:, :, cols] = grad.astype(jnp.bfloat16).reshape(images, rows, depth)

    for which, source in enumerate(sources):
        sent = source.at[:, :, pl.ds(0, width - local)]
        pltpu.make_async_copy(sent, sent, send_sem.at[which]).wait()
    sent = mixed.at[:, :, pl.ds(0, length - rows), :]
    pltpu.make_async_copy(sent, sent, back_send).wait()
    if gather:
        for kind, count in ((0, lines), (1, n), (2, 2 * n)):
            for j in range(2):
                sent = piece(j, 0, count)
                pltpu.make_async_copy(sent, sent, side_send.at[kind, j]).wait()

        def line_left(side, step, there):
            @pl.when(there)
            def _():
                for j in range(2):
                    sent = piece(j, 0)
                    pltpu.make_async_copy(sent, sent, line_send.at[side, step, j]).wait()

        for step in range(lines):
            line_left(0, step, jnp.logical_and(z - step >= 0, z + 1 < lines))
            line_left(1, step, jnp.logical_and(z + step < lines, z >= 1))


def shards(
    queries,
    keys,
    values,
    teacher,
    resample_index,
    resample_frac,
    timesteps,
    norm_gain,
    proj_in,
    bias_in,
    proj_out,
    bias_out,
):
    n, planes = lax.axis_size("seq"), lax.axis_size("dp")
    images, rows, width = queries.shape
    features = teacher.shape[2]
    hidden = proj_in.shape[1]
    gather = planes == 4 and n % 2 == 0 and proj_in.shape[0] % 16 == 0 and proj_out.shape[0] % 16 == 0
    if not gather:
        proj_in = lax.all_gather(proj_in, ("dp", "seq"), axis=0, tiled=True)
        proj_out = lax.all_gather(proj_out, ("dp", "seq"), axis=0, tiled=True)
    local = width // n
    chunk = min(local, 2 * HD)
    chunks = local // chunk
    length = rows * n
    band = teacher.shape[1]
    vmem = pl.BlockSpec(memory_space=pltpu.VMEM)
    smem = pl.BlockSpec(memory_space=pltpu.SMEM)
    hbm = pl.BlockSpec(memory_space=pl.ANY)
    dma = pltpu.SemaphoreType.DMA
    bf16, f32 = jnp.bfloat16, jnp.float32
    return pl.pallas_call(
        functools.partial(align_kernel, n, chunk, gather),
        out_shape=(
            jax.ShapeDtypeStruct((images, rows), f32),
            jax.ShapeDtypeStruct(queries.shape, bf16),
        ),
        in_specs=[hbm, hbm, hbm, hbm, vmem, vmem, smem, hbm, hbm, hbm, hbm, hbm],
        out_specs=(vmem, vmem),
        scratch_shapes=[
            pltpu.VMEM((3, images, chunks, length, chunk), bf16),
            pltpu.VMEM((images, chunks, length, chunk), bf16),
            pltpu.VMEM(queries.shape, bf16),
            pltpu.VMEM((images * rows, features), f32),
            pltpu.VMEM((images, band + 2 * HALO, features), bf16),
            pltpu.VMEM((width, hidden), bf16),
            pltpu.VMEM((hidden, features), bf16),
            pltpu.VMEM((1, width), f32),
            pltpu.VMEM((1, hidden), f32),
            pltpu.VMEM((1, features), f32),
            dma((3,)),
            dma((3, images, chunks)),
            dma,
            dma,
            dma((2,)),
            dma((2,)),
            dma,
            dma((3,)),
            dma((2,)),
            dma((2, planes * n if gather else 1)),
            dma((2, max(n // 2, 1), 2)),
            dma((3, 2)),
        ],
        compiler_params=pltpu.CompilerParams(
            collective_id=0, has_side_effects=True, vmem_limit_bytes=52 * 2**20
        ),
        name="align",
    )(
        queries, keys, values, teacher,
        jnp.transpose(resample_index, (0, 2, 1)), jnp.transpose(resample_frac, (0, 2, 1)),
        timesteps, norm_gain[None], bias_in[None], bias_out[None], proj_in, proj_out,
    )


def solution(mesh):
    return jax.shard_map(
        shards,
        mesh=mesh,
        in_specs=(
            P("dp", "seq", None),
            P("dp", "seq", None),
            P("dp", "seq", None),
            P("dp", "seq", None),
            P("dp", "seq", None),
            P("dp", "seq", None),
            P("dp"),
            P(),
            P(("dp", "seq"), None),
            P(),
            P(("dp", "seq"), None),
            P(),
        ),
        out_specs=(P("dp", "seq"), P("dp", "seq", None)),
        check_vma=False,
    )
```

time: 201 us -> 131 us (0.65)
  waiting for transfers between devices: 33.4 us -> 0 us
  Pallas kernels: 139 us -> 123 us
  between operations: 14.1 us -> 0.69 us
  local copies, waits for them, and re-layouts: 13.9 us -> 6.5 us
    all_gather x2 -> x0, waiting for transfers between devices: 32 us -> none  [the longest x1 32 us: shards(): full_in = lax.all_gather(proj_in, ('dp', 'seq'), axis=0, tiled=True)]
    pallas_call x2 -> x1, Pallas kernels: 139 us -> 123 us  [shards(): pl.pallas_call(functools.partial(align_kernel, n, chunk, gather), out_sha...]
    unnamed x18, local copies, waits for them, and re-layouts: 12.9 us -> 5.78 us
  transfers between devices with their start and end apart: 2 -> 0, of which waited for: 1 -> 0; matrix products, arithmetic and copies ran while one was open for 2% -> 0% of each run, Pallas kernels for 65% -> 0%
where the time goes in v2:
time: 131 us; the launch traced here: 130 us
  Pallas kernels  123 us (94%)
  local copies, waits for them, and re-layouts  6.5 us (5%)
    pallas_call x1, Pallas kernels, shards(): pl.pallas_call(functools.partial(align_kernel, n, chunk, gather), out_sha...  123 us
    unnamed x18, local copies, waits for them, and re-layouts  5.78 us

profile of v2, /device:TPU:0, one launch (start us, length us, event | category | flops | bytes accessed | tf_op | source)
XLA Modules:
  0.0 130.4 jit_solution(18039586918293748410)
XLA Ops:
  0.6 0.0 copy-start.3
  0.6 0.0 copy-start.4
  0.7 0.0 copy-start.7
  0.7 0.7 broadcast_in_dim.11.bias_out_hbm
  1.4 0.0 copy-done.3
  1.4 0.0 copy-done.4
  1.4 0.0 copy-done.7
  1.4 0.0 copy-start
  1.4 1.0 copy-done
  2.4 0.0 copy-start.1
  2.4 0.9 copy-done.1
  3.4 0.0 copy-start.2
  3.4 0.9 copy-done.2
  4.3 0.0 copy-start.5
  4.3 0.7 copy-done.5
  5.0 0.0 copy-start.6
  5.0 0.7 copy-done.6
  5.6 123.2 %align.1 = (f32[2,64]{1,0:T(2,128)S(1)}, bf16[2,64,4096]{2,1,0:T(8,128)(2,1)S(1)}) custom-call(bf16[2,64,4096]{2,1,0:T(8,128)(2,1)} %q_ref.1, bf16[2,64,4096]{2,1,0:T(8,128)(2,1)} %k_ref.1, bf16[2,64,4096]{2,1,0:T(8,128)(2,1)} %v_ref.1, bf16[2,80,1536]{2,1,0:T(8,128)(2,1)S(1)} %copy-done, s32[2,4,64]{2,1,0:T(4,128)S(1)} %bitcast.5, s32[2,2,64]{2,1,0:T(2,128)S(1)} %bitcast.7, ...), custom_call_target="tpu_custom_call" | custom-call | tf_op jit(solution)/shard_map/align/pallas_call | solution.py:399
  128.9 0.6 copy.16
  129.5 1.0 copy.17
Async XLA Ops:
  0.6 0.8 copy-start.3
  0.6 0.7 copy-start.4
  0.7 0.7 copy-start.7
  1.4 1.0 copy-start
  2.4 0.9 copy-start.1
  3.4 0.9 copy-start.2
  4.3 0.7 copy-start.5
  5.0 0.7 copy-start.6

commit v3 on v2

--- a/solution.py
+++ b/solution.py
@@ -36,6 +36,10 @@
     band = t_ref.shape[1]
     reach = band + 2 * HALO
     right, left = lax.rem(me + 1, n), lax.rem(me + n - 1, n)
+
+    def peer(step):
+        return lax.bitwise_xor(me, step) if n & (n - 1) == 0 else lax.rem(me + step, n)
+
     here = dp * n + me
     weights = ((in_ref, in_hbm.shape[0]), (out_ref, out_hbm.shape[0]))
 
@@ -187,7 +191,7 @@
 
         @pl.loop(1, n)
         def _(step):
-            to = lax.rem(me + step, n)
+            to = peer(step)
             for which, source in enumerate(sources):
                 pltpu.make_async_remote_copy(
                     src_ref=source.at[image, :, columns(to, part)],
@@ -265,7 +269,7 @@
 
         @pl.loop(1, n)
         def _(step, image=image, part=part):
-            to = lax.rem(me + step, n)
+            to = peer(step)
             pltpu.make_async_remote_copy(
                 src_ref=mixed.at[image, part, pl.ds(pl.multiple_of(to * rows, rows), rows), :],
                 dst_ref=att_ref.at[image, :, columns(me, part)],
@@ -393,7 +397,7 @@
     band = teacher.shape[1]
     vmem = pl.BlockSpec(memory_space=pltpu.VMEM)
     smem = pl.BlockSpec(memory_space=pltpu.SMEM)
-    hbm = pl.BlockSpec(memory_space=pl.ANY)
+    hbm = pl.BlockSpec(memory_space=pltpu.HBM)
     dma = pltpu.SemaphoreType.DMA
     bf16, f32 = jnp.bfloat16, jnp.float32
     return pl.pallas_call(
@@ -429,7 +433,7 @@
             dma((3, 2)),
         ],
         compiler_params=pltpu.CompilerParams(
-            collective_id=0, has_side_effects=True, vmem_limit_bytes=52 * 2**20
+            collective_id=0, has_side_effects=True, vmem_limit_bytes=60 * 2**20
         ),
         name="align",
     )(

time: 131 us -> 130 us (level)
  local copies, waits for them, and re-layouts: 6.5 us -> 4.79 us
    unnamed x18 -> x4, local copies, waits for them, and re-layouts: 5.78 us -> 3.5 us
where the time goes in v3:
time: 130 us
  Pallas kernels  124 us (95%)
  local copies, waits for them, and re-layouts  4.79 us (4%)
    pallas_call x1, Pallas kernels, shards(): pl.pallas_call(functools.partial(align_kernel, n, chunk, gather), out_sha...  124 us
    unnamed x4, local copies, waits for them, and re-layouts  3.5 us

profile of v3, /device:TPU:0, one launch (start us, length us, event | category | flops | bytes accessed | tf_op | source)
XLA Modules:
  0.0 129.9 jit_solution(15130152410425642458)
XLA Ops:
  0.6 1.3 broadcast_in_dim.11.bias_out_hbm
  1.9 124.4 %align.1 = (f32[2,64]{1,0:T(2,128)}, bf16[2,64,4096]{2,1,0:T(8,128)(2,1)}) custom-call(bf16[2,64,4096]{2,1,0:T(8,128)(2,1)} %q_ref.1, bf16[2,64,4096]{2,1,0:T(8,128)(2,1)} %k_ref.1, bf16[2,64,4096]{2,1,0:T(8,128)(2,1)} %v_ref.1, bf16[2,80,1536]{2,1,0:T(8,128)(2,1)} %t_ref.1, s32[2,4,64]{2,1,0:T(4,128)} %bitcast.5, s32[2,2,64]{2,1,0:T(2,128)} %bitcast.7, ...), custom_call_target="tpu_custom_call" | custom-call | tf_op jit(solution)/shard_map/align/pallas_call | solution.py:403
  126.4 0.0 copy-start
  126.4 0.6 copy-done
  127.0 0.6 copy.16
  127.6 2.3 %copy.17 = bf16[2,64,4096]{2,1,0:T(8,128)(2,1)} copy(bf16[2,64,4096]{2,1,0:T(8,128)(2,1)} %get-tuple-element.5) | data formatting | bytes 2097152
Async XLA Ops:
  126.4 0.7 copy-start
